TPU v7x, 768 devices: a whole 4x8x12 slice. The times are simulated.
768 devices in a mesh: fn: 24 (over z, core), blk: 32 (over y, x).
Axes of the slice: x: 4, y: 8, z: 12, core: 2. Of those that a mesh axis runs over, the one named last changes fastest.
Arguments:
- orbitals: bfloat16 [6144, 32768], P('fn', 'blk'), may hold values from -1 to 1
- potential: float32 [24, 32768], P('fn', 'blk'), may hold values from 0.5 to 2
- zone_of: int32 [6144, 1], P('fn'), may hold values from 0 to 23; in each aligned block of 256 rows (0 to 255, 256 to 511, ...) at most 24 rows name the same one
- chem_shift: float32 [1], replicated, may hold values from 0.9 to 1.6
Outputs:
- intersection: float32 [24, 576, 576], P('fn', 'blk')
- hamiltonian: float32 [24, 576, 576], P('fn', 'blk')
- kernel: float32 [24, 576, 576], P('fn', 'blk')
Inputs may be any that keep to these rules, and one draw needn't show every extreme that they name: `zone_of`: among the 256 functions of one index of fn (aligned blocks of rows) no zone is named more than 24 times, and in some block one zone is named exactly 24 times; every zone is named somewhere.
All inputs are finite; a program needn't handle non-finite values.
Results may differ from a plain program's by a relative error of at most 0.00074.
Values may be sent and summed in bfloat16 or wider, within the bound.
A program may use at most 32 MiB of HBM per device.

v0:
```python
import jax
import jax.numpy as jnp
from jax import lax
from jax.sharding import PartitionSpec as P

SLOTS = 576


def add_product(left_rows, shard_rows):
    return jnp.dot(
        left_rows, shard_rows, precision=lax.Precision.HIGHEST, preferred_element_type=jnp.float32
    )


def start_kernel(intersection_part, hamilton_part, row_ids, present, mu_value):
    diagonal = (row_ids[:, None] == jnp.arange(SLOTS, dtype=jnp.int32)[None, :]).astype(
        jnp.float32
    ) * present[None, :]
    return 0.5 * diagonal - 0.5 * (hamilton_part - mu_value * intersection_part)


def on_device(orbitals, potential, zone_of, chem_shift):
    zone_count = lax.axis_size("fn")
    stripe_count = lax.axis_size("blk")
    capacity = SLOTS // zone_count
    row_count = SLOTS // stripe_count
    first_row = lax.axis_index("blk") * row_count
    slab_width = orbitals.shape[1]
    mu_value = chem_shift[0]
    highest = lax.Precision.HIGHEST
    zone_ids = zone_of[:, 0]
    onehot = (zone_ids[:, None] == jnp.arange(zone_count, dtype=jnp.int32)[None, :]).astype(
        jnp.int32
    )
    rank_in = jnp.sum((jnp.cumsum(onehot, axis=0) - onehot) * onehot, axis=1)
    target = zone_ids * capacity + rank_in
    slotted = (
        jnp.zeros((SLOTS, slab_width), jnp.bfloat16)
        .at[target]
        .set(orbitals)
        .reshape(zone_count, capacity, slab_width)
    )
    filled = (
        jnp.zeros((SLOTS,), jnp.bfloat16)
        .at[target]
        .set(jnp.ones(zone_ids.shape, jnp.bfloat16))
        .reshape(zone_count, capacity)
    )
    levels = lax.all_gather(potential, "fn", axis=0, tiled=True)
    owner_pot = jnp.dot(
        onehot.astype(jnp.float32), levels, precision=highest, preferred_element_type=jnp.float32
    )
    weighted_own = (owner_pot * orbitals.astype(jnp.float32)).astype(jnp.bfloat16)
    weighted_slots = (
        jnp.zeros((SLOTS, slab_width), jnp.bfloat16)
        .at[target]
        .set(weighted_own)
        .reshape(zone_count, capacity, slab_width)
    )
    coeffs, weighted, marks = (
        lax.all_to_all(slotted, "fn", split_axis=0, concat_axis=0, tiled=True),
        lax.all_to_all(weighted_slots, "fn", split_axis=0, concat_axis=0, tiled=True),
        lax.all_to_all(filled, "fn", split_axis=0, concat_axis=0, tiled=True),
    )
    coeffs = coeffs.reshape(SLOTS, slab_width)
    weighted = weighted.reshape(SLOTS, slab_width)
    present = marks.reshape(SLOTS).astype(jnp.float32)
    stacked = jnp.concatenate([coeffs, weighted], axis=0)
    row_ids = first_row + jnp.arange(row_count, dtype=jnp.int32)
    joined = lax.psum_scatter(
        lax.dot_general(
            coeffs, stacked, (((1,), (1,)), ((), ())), preferred_element_type=jnp.float32
        ),
        "blk",
        scatter_dimension=0,
        tiled=True,
    )
    intersection_part = joined[:, :SLOTS]
    hamilton_part = joined[:, SLOTS:]
    kernel_part = start_kernel(intersection_part, hamilton_part, row_ids, present, mu_value)
    product = add_product(kernel_part, lax.all_gather(intersection_part, "blk", axis=0, tiled=True))
    square = add_product(product, lax.all_gather(kernel_part, "blk", axis=0, tiled=True))
    cubed = add_product(product, lax.all_gather(square, "blk", axis=0, tiled=True))
    kernel = 3.0 * square - 2.0 * cubed
    return (intersection_part[None], hamilton_part[None], kernel[None])


def solution(mesh):
    placed = (P("fn", "blk"), P("fn", "blk"), P("fn", None), P())
    return jax.shard_map(
        on_device,
        mesh=mesh,
        in_specs=placed,
        out_specs=(P("fn", "blk", None), P("fn", "blk", None), P("fn", "blk", None)),
        check_vma=False,
    )
```

profile of v0, /device:TPU:1, one launch (start us, length us, event | category | flops | bytes accessed | tf_op | source)
XLA Modules:
  0.0 596.7 jit_solution(18116711851682990049)
XLA Ops:
  7.2 0.7 fusion.15
  7.9 0.6 reduce-window.6
  8.4 0.2 slice_reduce_fusion
  8.7 0.8 fusion.14
  9.4 0.7 compare_select_fusion
  10.1 3.2 scatter_custom_fusion
  13.3 0.0 copy-start.4
  13.3 16.8 %all-to-all-start = ((bf16[24,24,1024]{2,1,0:T(8,128)(2,1)}), bf16[24,24,1024]{2,1,0:T(8,128)(2,1)S(1)}, u32[]{:S(2)}, u32[]{:S(2)}) async-start(bf16[24,24,1024]{2,1,0:T(8,128)(2,1)} %bitcast.5), calls=%async_computation | async-start | bytes 2359296 | tf_op jit(solution)/shard_map/all_to_all | solution.py:61
  30.2 0.0 all-reduce.3.cloned.1.call-start
  30.2 0.0 copy-done.4
  30.2 58.8 %all-gather = f32[24,1,1024]{2,1,0:T(1,128)S(1)} all-gather(f32[1,1,1024]{2,1,0:T(1,128)S(1)} %bitcast.50), channel_id=1, replica_groups=mesh['fn'=24,'blk'=32] {'fn'}, dimensions={0}, use_global_device_ids=true | all-gather | bytes 102400 | tf_op jit(solution)/shard_map/all_gather | solution.py:49
  89.1 0.0 copy-done.2
  89.1 0.0 copy-done.3
  89.1 1.0 fusion.4
  90.1 2.0 scatter_custom_fusion.1
  92.1 0.0 all-to-all-done
  92.1 49.7 %all_to_all.20 = bf16[24,24,1024]{2,1,0:T(8,128)(2,1)S(1)} all-to-all(bf16[24,24,1024]{2,1,0:T(8,128)(2,1)S(1)} %bitcast.42), channel_id=1, replica_groups=mesh['fn'=24,'blk'=32] {'fn'}, dimensions={0} | all-to-all | bytes 2359296 | tf_op jit(solution)/shard_map/all_to_all | solution.py:62
  141.9 3.2 fusion
  145.1 0.0 all-reduce.3.cloned.1.call-update
  145.1 2.2 scatter_custom_fusion.2
  147.3 0.7 all_to_all.16
  148.0 6.1 %all-to-all-start.2 = ((bf16[24,1,24]{2,1,0:T(2,128)(2,1)}), bf16[24,1,24]{2,1,0:T(2,128)(2,1)S(1)}, u32[]{:S(2)}, u32[]{:S(2)}) async-start(bf16[24,1,24]{2,1,0:T(2,128)(2,1)} %all_to_all.16), calls=%async_computation.2 | async-start | bytes 24576 | tf_op jit(solution)/shard_map/all_to_all | solution.py:63
  154.1 0.0 all-gather.8.cloned.1.call-start
  154.8 1.3 dynamic-slice
  156.7 6.8 %all-to-all-done.2 = bf16[24,1,24]{2,1,0:T(2,128)(2,1)S(1)} async-done(((bf16[24,1,24]{2,1,0:T(2,128)(2,1)}), bf16[24,1,24]{2,1,0:T(2,128)(2,1)S(1)}, u32[]{:S(2)}, u32[]{:S(2)}) %all-to-all-start.2) | async-done | bytes 1184 | tf_op jit(solution)/shard_map/all_to_all | solution.py:63
  163.6 0.1 reshape.57
  163.7 152.4 %all-reduce.3.cloned.1.call-done = f32[576,1152]{1,0:T(8,128)} async-done(((f32[576,1152]{1,0:T(8,128)}), f32[576,1152]{1,0:T(8,128)}) %all-reduce.3.cloned.1.call-update) | async-done | bytes 2654224
  316.1 1.7 fusion.20
  317.8 0.0 all-gather.8.cloned.1.call-update
  317.8 0.0 all-gather.10.cloned.1.call-start
  317.8 0.7 all-gather.10.cloned.1.call-update
  318.5 0.2 all-gather.12.cloned.1.call-start
  318.7 87.2 %all-gather.8.cloned.1.call-done = f32[32,18,576]{2,1,0:T(8,128)} async-done(((f32[1,18,576]{2,1,0:T(8,128)}), f32[32,18,576]{2,1,0:T(8,128)}) %all-gather.8.cloned.1.call-update) | async-done | bytes 1327120 | tf_op jit(solution)/shard_map/all_gather | solution.py:81
  405.9 1.6 reshape.85
  407.5 88.3 %all-gather.10.cloned.1.call-done = f32[32,18,576]{2,1,0:T(8,128)} async-done(((f32[1,18,576]{2,1,0:T(8,128)}), f32[32,18,576]{2,1,0:T(8,128)}) %all-gather.10.cloned.1.call-update) | async-done | bytes 1327120 | tf_op jit(solution)/shard_map/all_gather | solution.py:82
  495.9 1.6 reshape.87
  497.4 0.0 copy-start
  497.5 1.8 fusion.21
  499.3 1.5 fusion.22
  500.8 0.0 all-gather.12.cloned.1.call-update
  500.8 0.0 copy-done
  500.8 0.7 copy.16
  501.5 0.7 copy.17
  502.2 84.9 %all-gather.12.cloned.1.call-done = f32[32,18,576]{2,1,0:T(8,128)} async-done(((f32[1,18,576]{2,1,0:T(8,128)}), f32[32,18,576]{2,1,0:T(8,128)}) %all-gather.12.cloned.1.call-update) | async-done | bytes 1327120 | tf_op jit(solution)/shard_map/all_gather | solution.py:83
  587.1 1.6 reshape.89
  588.7 0.0 copy-done.1
  588.7 0.9 fusion.6
  589.5 0.7 copy.18
  (8 shorter events, 0.1 us)
Async XLA Ops:
  13.3 16.9 %copy-start.4 = (f32[1,1024]{1,0:T(1,128)S(1)}, f32[1,1024]{1,0:T(1,128)}, u32[]{:S(2)}) copy-start(f32[1,1024]{1,0:T(1,128)} %param.5) | copy-start | bytes 12292
  13.3 75.7 %copy-start.2 = (bf16[256,1024]{1,0:T(8,128)(2,1)S(1)}, bf16[256,1024]{1,0:T(8,128)(2,1)}, u32[]{:S(2)}) copy-start(bf16[256,1024]{1,0:T(8,128)(2,1)} %param.4) | copy-start | bytes 1572868
  13.3 75.7 %copy-start.3 = (s32[256,1]{0,1:T(1,128)S(1)}, s32[256,1]{0,1:T(1,128)}, u32[]{:S(2)}) copy-start(s32[256,1]{0,1:T(1,128)} %param.6) | copy-start | bytes 3076
  13.3 78.8 %all-to-all-start = ((bf16[24,24,1024]{2,1,0:T(8,128)(2,1)}), bf16[24,24,1024]{2,1,0:T(8,128)(2,1)S(1)}, u32[]{:S(2)}, u32[]{:S(2)}) async-start(bf16[24,24,1024]{2,1,0:T(8,128)(2,1)} %bitcast.5), calls=%async_computation | async-start | bytes 2359296 | tf_op jit(solution)/shard_map/all_to_all | solution.py:61
  30.2 285.9 %all-reduce.3.cloned.1.call-start = ((), (), s32[]{:S(2)}) async-start(), calls=%async_computation.6 | async-start | bytes 5308416
  148.0 15.5 %all-to-all-start.2 = ((bf16[24,1,24]{2,1,0:T(2,128)(2,1)}), bf16[24,1,24]{2,1,0:T(2,128)(2,1)S(1)}, u32[]{:S(2)}, u32[]{:S(2)}) async-start(bf16[24,1,24]{2,1,0:T(2,128)(2,1)} %all_to_all.16), calls=%async_computation.2 | async-start | bytes 24576 | tf_op jit(solution)/shard_map/all_to_all | solution.py:63
  154.1 251.9 %all-gather.8.cloned.1.call-start = ((), (), s32[]{:S(2)}) async-start(), calls=%async_computation.3 | async-start | bytes 2027520 | tf_op jit(solution)/shard_map/all_gather | solution.py:81
  317.8 178.1 %all-gather.10.cloned.1.call-start = ((), (), s32[]{:S(2)}) async-start(), calls=%async_computation.4 | async-start | bytes 2027520 | tf_op jit(solution)/shard_map/all_gather | solution.py:82
  318.5 268.6 %all-gather.12.cloned.1.call-start = ((), (), s32[]{:S(2)}) async-start(), calls=%async_computation.5 | async-start | bytes 2027520 | tf_op jit(solution)/shard_map/all_gather | solution.py:83
  497.4 3.4 copy-start
  502.2 86.5 %copy-start.1 = (f32[18,576]{1,0:T(8,128)S(1)}, f32[18,576]{1,0:T(8,128)}, u32[]{:S(2)}) copy-start(f32[18,576]{1,0:T(8,128)} %fusion.22) | copy-start | bytes 124420
Sparse Core Ops, SparseCore 0:
  145.3 170.7 all-reduce.2
  319.8 86.0 all-gather.7
  409.7 86.1 all-gather.9
  500.9 86.0 all-gather.11
where the time goes:
time: 600 us; the launch traced here: 597 us
  waiting for transfers between devices  420 us (70%)
  blocking collectives  109 us (18%)
  starting transfers between devices  23.2 us (4%)
  local copies, waits for them, and re-layouts  16.3 us (3%)
  between operations  15.2 us (3%)
  matrix products  8.47 us (1%)
    unnamed x5, waiting for transfers between devices  153 us
    all_gather x1, waiting for transfers between devices, on_device(): lax.all_gather(kernel_part, 'blk', axis=0, tiled=True)  88.3 us
    all_gather x1, waiting for transfers between devices, on_device(): lax.all_gather(intersection_part, 'blk', axis=0, tiled=True)  87.2 us
    all_gather x1, waiting for transfers between devices, on_device(): lax.all_gather(square, 'blk', axis=0, tiled=True)  84.9 us
    all_gather x1, blocking collectives, on_device(): levels = lax.all_gather(potential, 'fn', axis=0, tiled=True)  58.8 us
    all_to_all x1, blocking collectives, on_device(): lax.all_to_all(weighted_slots, 'fn', split_axis=0, concat_axis=0, tiled=T...  49.7 us
    all_to_all x1, starting transfers between devices, on_device(): lax.all_to_all(slotted, 'fn', split_axis=0, concat_axis=0, tiled=True)  16.8 us
  transfers between devices with their start and end apart: 6, of which 5 were waited for; matrix products, arithmetic and copies ran while one was open for 2% of the time, Pallas kernels for 0%

commit v1 on v0

v1 whole, which is shorter than its diff:
```python
import jax
import jax.numpy as jnp
from jax import lax
from jax.experimental import pallas as pl
from jax.experimental.pallas import tpu as pltpu
from jax.sharding import PartitionSpec as P

SLOTS = 576
WIDE = 640
LANES = 128
NX = 4
CORES = 2
BIG = 2.0**100
BF16 = jnp.bfloat16
F32 = jnp.float32

STRIP_ROWS = [SLOTS - LANES * j for j in range(5)]
STRIP_AT = [sum(STRIP_ROWS[:j]) for j in range(5)]
TRIANGLE = sum(STRIP_ROWS)


def wrap(value, n):
    return lax.rem(value + n, n)


def rows(start, count):
    return pl.ds(pl.multiple_of(start, 8), count)


def near_first(k):
    return ((k + 1) // 2) * (2 * lax.rem(k, 2) - 1)


def first_part(count):
    return (count // 2 + 7) // 8 * 8


def split(value):
    high = value.astype(BF16)
    return high, (value - high.astype(F32)).astype(BF16)


def times(left, right_high, right_low):
    high, low = split(left)
    count = left.shape[0]
    both = jnp.dot(
        jnp.concatenate([high, low], axis=0), right_high[...], preferred_element_type=F32
    )
    return both[:count] + both[count:] + jnp.dot(high, right_low[...], preferred_element_type=F32)


class Ring:
    def __init__(self, n, me, device, base, size):
        self.n, self.me, self.device, self.base, self.size = n, me, device, base, size
        self.hops = n // 2
        self.part = first_part(size)

    def at(self, offset):
        return self.base + wrap(self.me + offset, self.n) * self.size


def cut(ring, way, whole):
    if whole:
        return 0, ring.size
    return (0, ring.part) if way > 0 else (ring.part, ring.size - ring.part)


def ring_sum(ring, data, landing, send_sem, recv_sem):
    copies = {}

    def send(t, way):
        skip, count = cut(ring, way, t > 0)
        d = 0 if way > 0 else 1
        copies[t, way] = pltpu.make_async_remote_copy(
            src_ref=data.at[rows(ring.at(way * (ring.hops - t)) + skip, count)],
            dst_ref=landing.at[d, t, pl.ds(skip, count)],
            send_sem=send_sem.at[d, t],
            recv_sem=recv_sem.at[d, t],
            device_id=ring.device(wrap(ring.me + way, ring.n)),
        )
        copies[t, way].start()

    def add(t, way):
        copies[t, way].wait_recv()
        skip, count = cut(ring, way, t > 0)
        here = rows(ring.at(way * (ring.hops - t - 1)) + skip, count)
        data[here, :] += landing[0 if way > 0 else 1, t, pl.ds(skip, count), :]

    def step(t):
        def run():
            for way in (1, -1):
                if t > 0:
                    add(t - 1, way)
                if t < ring.hops:
                    send(t, way)

        return run

    return [step(t) for t in range(ring.hops + 1)], copies


def ring_gather(ring, data, send_sem, recv_sem):
    sent = []

    def copy(t, way, offset):
        skip, count = cut(ring, way, t < ring.hops - 1)
        d = 0 if way > 0 else 1
        here = data.at[rows(ring.at(offset) + skip, count)]
        return pltpu.make_async_remote_copy(
            src_ref=here,
            dst_ref=here,
            send_sem=send_sem.at[d, t],
            recv_sem=recv_sem.at[d, t],
            device_id=ring.device(wrap(ring.me + way, ring.n)),
        )

    def step(t):
        def run():
            for way in (1, -1):
                if t > 0:
                    copy(t - 1, way, -way * t).wait_recv()
                if t < ring.hops:
                    out = copy(t, way, -way * t)
                    out.start()
                    sent.append(out)

        return run

    return [step(t) for t in range(ring.hops + 1)], sent


def direct_sum(ring, data, total, landing, send_sem, recv_sem):
    copies = []

    def start():
        for k in range(1, ring.n):
            copies.append(
                pltpu.make_async_remote_copy(
                    src_ref=data.at[rows(ring.at(k), ring.size)],
                    dst_ref=landing.at[k - 1],
                    send_sem=send_sem.at[k - 1],
                    recv_sem=recv_sem.at[k - 1],
                    device_id=ring.device(wrap(ring.me + k, ring.n)),
                )
            )
            copies[-1].start()

    def finish():
        here = rows(ring.at(0), ring.size)
        value = data[here, :]
        for k in range(1, ring.n):
            copies[k - 1].wait_recv()
            value = value + landing[k - 1]
        total[here, :] = value

    return start, finish, copies


def direct_gather(ring, data, send_sem, recv_sem):
    sent = []

    def copy(k, offset):
        here = data.at[rows(ring.at(offset), ring.size)]
        return pltpu.make_async_remote_copy(
            src_ref=here,
            dst_ref=here,
            send_sem=send_sem.at[k - 1],
            recv_sem=recv_sem.at[k - 1],
            device_id=ring.device(wrap(ring.me + k, ring.n)),
        )

    def start():
        for k in range(1, ring.n):
            sent.append(copy(k, 0))
            sent[-1].start()

    def finish():
        for k in range(1, ring.n):
            copy(k, -k).wait_recv()

    return start, finish, sent


def kernel(
    n_fn, ny, size_a, size_b,
    zone_ref, orb_ref, pot_ref, mu_ref, s_out, h_out, k_out,
    send, recv, coeffs, weighted, present, part, gath,
    land_ya, land_xa, land_xb, land_yb,
    s_full, h_full, l_full, s_high, s_low, l_high, l_low, l_rows,
    z_send, z_recv, sum_ya, sum_xa, sum_xb, sum_yb, get_ya, get_xa, get_xb, get_yb,
):
    cap = SLOTS // n_fn
    nz = n_fn // CORES
    me = lax.axis_index("fn")
    blk = lax.axis_index("blk")
    my_z, core = me // CORES, lax.rem(me, CORES)
    y, x = blk // NX, lax.rem(blk, NX)

    def along_y(pos):
        return {"blk": pos * NX + x}

    def along_x(pos):
        return {"blk": y * NX + pos}

    def fn_index(dz, dc):
        return wrap(my_z + dz, nz) * CORES + lax.rem(core + dc, CORES)

    barrier = pltpu.get_barrier_semaphore()

    @pl.loop(1, n_fn)
    def _(k):
        pl.semaphore_signal(barrier, inc=1, device_id={"fn": wrap(me + k - n_fn, n_fn)})

    for k in range(1, ny):
        pl.semaphore_signal(barrier, inc=1, device_id=along_y(wrap(y + k, ny)))
    for k in range(1, NX):
        pl.semaphore_signal(barrier, inc=1, device_id=along_x(wrap(x + k, NX)))

    funcs = orb_ref.shape[0]
    zones = zone_ref[...]
    onehot = (zones == lax.broadcasted_iota(jnp.int32, (n_fn, funcs), 0)).astype(F32)
    earlier = (
        lax.broadcasted_iota(jnp.int32, (funcs, funcs), 0)
        < lax.broadcasted_iota(jnp.int32, (funcs, funcs), 1)
    ).astype(F32)
    before = jnp.dot(onehot.astype(BF16), earlier.astype(BF16), preferred_element_type=F32)
    rank = jnp.sum(before * onehot, axis=0, keepdims=True).astype(jnp.int32)
    target = zones * cap + rank
    selector = (target == lax.broadcasted_iota(jnp.int32, (SLOTS, funcs), 0)).astype(F32)
    filled = jnp.sum(selector, axis=1, keepdims=True) > 0.5
    selector = selector.astype(BF16)
    slab = orb_ref.shape[1]
    for c0 in range(0, slab, 256):
        slotted = jnp.dot(selector, orb_ref[:, c0 : c0 + 256], preferred_element_type=F32)
        if c0 == 0:
            slotted = jnp.where(filled, slotted, BIG)
        for zone in range(n_fn):
            send[zone, :, c0 : c0 + 256] = slotted[zone * cap : (zone + 1) * cap].astype(BF16)

    pl.semaphore_wait(barrier, n_fn - 1 + ny - 1 + NX - 1)

    def z_copy(k, dc, dz_from):
        dz = near_first(k)
        q = CORES * k + dc - 1
        to = fn_index(dz, dc)
        return pltpu.make_async_remote_copy(
            src_ref=send.at[to],
            dst_ref=recv.at[fn_index(dz_from * dz, dc) if dz_from else me],
            send_sem=z_send.at[q],
            recv_sem=z_recv.at[q],
            device_id={"fn": to},
        )

    z_copy(0, 1, 0).start()

    @pl.loop(1, nz)
    def _(k):
        for dc in range(CORES):
            z_copy(k, dc, 0).start()

    recv[me] = send[me]
    coeffs[SLOTS:, :] = jnp.zeros((WIDE - SLOTS, slab), BF16)
    weighted[SLOTS:, :] = jnp.zeros((WIDE - SLOTS, slab), BF16)
    if part.shape[0] > 2 * TRIANGLE:
        part[2 * TRIANGLE :, :] = jnp.zeros((part.shape[0] - 2 * TRIANGLE, LANES), F32)
    potential = pot_ref[...]

    def unpack(dz):
        chip = wrap(my_z - dz, nz)
        value = jnp.concatenate(
            [recv[chip * CORES + c].astype(F32) for c in range(CORES)], axis=0
        )
        marks = value[:, :1] < 0.5 * BIG
        value = jnp.where(marks, value, 0.0)
        here = pl.ds(pl.multiple_of(chip * (CORES * cap), 16), CORES * cap)
        coeffs[here, :] = value.astype(BF16)
        weighted[here, :] = (potential * value).astype(BF16)
        present[here, :] = jnp.broadcast_to(marks.astype(F32), (CORES * cap, LANES))

    z_copy(0, 1, -1).wait_recv()
    unpack(0)

    @pl.loop(1, nz)
    def _(k):
        for dc in range(CORES):
            z_copy(k, dc, -1).wait_recv()
        unpack(near_first(k))

    def outer(left, right, j, width):
        return lax.dot_general(
            left[LANES * j : SLOTS, :],
            right[LANES * j : LANES * j + width, :],
            (((1,), (1,)), ((), ())),
            preferred_element_type=F32,
        )

    def store(value, at, j):
        part[at + STRIP_AT[j] : at + STRIP_AT[j] + STRIP_ROWS[j], :] = value

    for j, width in ((0, 256), (2, 256), (4, 128)):
        gram = outer(coeffs, coeffs, j, width)
        ham = 0.5 * (outer(coeffs, weighted, j, width) + outer(weighted, coeffs, j, width))
        for at, value in ((0, gram), (TRIANGLE, ham)):
            store(value[:, :LANES], at, j)
            if width > LANES:
                store(value[LANES:, LANES:], at, j + 1)

    base_b = ny * NX * size_a
    ring_ya = Ring(ny, y, along_y, 0, NX * size_a)
    ring_xa = Ring(NX, x, along_x, y * (NX * size_a), size_a)
    ring_xb = Ring(NX, x, along_x, base_b, ny * size_b)
    ring_yb = Ring(ny, y, along_y, base_b + x * (ny * size_b), size_b)
    ya, sent_ya = ring_sum(ring_ya, part, land_ya, sum_ya.at[0], sum_ya.at[1])
    xb, sent_xb = ring_sum(ring_xb, part, land_xb, sum_xb.at[0], sum_xb.at[1])
    xa_start, xa_finish, sent_xa = direct_sum(
        ring_xa, part, gath, land_xa, sum_xa.at[0], sum_xa.at[1]
    )
    yb_start, yb_finish, sent_yb = direct_sum(
        ring_yb, part, gath, land_yb, sum_yb.at[0], sum_yb.at[1]
    )
    ga_start, ga_finish, sent_ga = direct_gather(ring_xa, gath, get_xa.at[0], get_xa.at[1])
    gb_start, gb_finish, sent_gb = direct_gather(ring_yb, gath, get_yb.at[0], get_yb.at[1])
    gya, sent_gya = ring_gather(ring_ya, gath, get_ya.at[0], get_ya.at[1])
    gxb, sent_gxb = ring_gather(ring_xb, gath, get_xb.at[0], get_xb.at[1])

    def merged(a, b):
        keyed = [((i + 0.5) / len(a), 0, s) for i, s in enumerate(a)]
        keyed += [((i + 0.5) / len(b), 1, s) for i, s in enumerate(b)]
        for _, _, s in sorted(keyed, key=lambda item: item[:2]):
            s()

    merged(ya[:-1], xb[:-1])
    xb[-1]()
    yb_start()
    ya[-1]()
    xa_start()
    xa_finish()
    ga_start()
    yb_finish()
    gb_start()
    ga_finish()
    gya[0]()
    gb_finish()
    gxb[0]()
    merged(gya[1:], gxb[1:])

    mu = mu_ref[0]
    eye = (
        lax.broadcasted_iota(jnp.int32, (LANES, LANES), 0)
        == lax.broadcasted_iota(jnp.int32, (LANES, LANES), 1)
    ).astype(F32)
    for i in range(5):
        high = min(LANES, SLOTS - LANES * i)
        for j in range(i + 1):
            at = STRIP_AT[j] + LANES * (i - j)
            s_block = gath[at : at + high, :]
            h_block = gath[TRIANGLE + at : TRIANGLE + at + high, :]
            l_block = -0.5 * (h_block - mu * s_block)
            if i == j:
                l_block = l_block + 0.5 * eye[:high] * present[LANES * i : LANES * i + high, :]
            for block, full in ((s_block, s_full), (h_block, h_full), (l_block, l_full)):
                if high < LANES:
                    block = jnp.concatenate([block, jnp.zeros((LANES - high, LANES), F32)], axis=0)
                full[LANES * i : LANES * (i + 1), LANES * j : LANES * (j + 1)] = block
                if i > j:
                    full[LANES * j : LANES * (j + 1), LANES * i : LANES * (i + 1)] = block.T

    first = blk * s_out.shape[1]
    l_rows[...] = jnp.zeros(l_rows.shape, F32)
    for i in range(s_out.shape[1]):
        s_out[0, i : i + 1, :] = s_full[pl.ds(first + i, 1), :][:, :SLOTS]
        h_out[0, i : i + 1, :] = h_full[pl.ds(first + i, 1), :][:, :SLOTS]
        l_rows[i : i + 1, :] = l_full[pl.ds(first + i, 1), :]
    for i in range(5):
        here = slice(LANES * i, LANES * (i + 1))
        s_high[here, :], s_low[here, :] = split(s_full[here, :])
        l_high[here, :], l_low[here, :] = split(l_full[here, :])

    product = times(l_rows[...], s_high, s_low)
    square = times(product, l_high, l_low)
    cubed = times(times(square, s_high, s_low), l_high, l_low)
    k_out[0] = (3.0 * square - 2.0 * cubed)[: k_out.shape[1], :SLOTS]

    z_copy(0, 1, 0).wait_send()

    @pl.loop(1, nz)
    def _(k):
        for dc in range(CORES):
            z_copy(k, dc, 0).wait_send()

    sent = list(sent_ya.values()) + list(sent_xb.values())
    for copy in sent + sent_xa + sent_yb + sent_ga + sent_gb + sent_gya + sent_gxb:
        copy.wait_send()


def on_device(orbitals, potential, zone_of, chem_shift):
    n_fn = lax.axis_size("fn")
    n_blk = lax.axis_size("blk")
    ny = n_blk // NX
    cap = SLOTS // n_fn
    funcs, slab = orbitals.shape
    count = SLOTS // n_blk
    each = -(-2 * TRIANGLE // (n_blk * 8)) * 8
    size_a = each * 6 // 13 // 8 * 8
    size_b = each - size_a

    def sems(*shape):
        return pltpu.SemaphoreType.DMA((2,) + shape)

    hy, hx = ny // 2, NX // 2
    out = jax.ShapeDtypeStruct((1, count, SLOTS), F32)
    vmem = pl.BlockSpec(memory_space=pltpu.VMEM)

    def body(*refs):
        kernel(n_fn, ny, size_a, size_b, *refs)

    return pl.pallas_call(
        body,
        out_shape=(out, out, out),
        in_specs=[vmem, vmem, vmem, pl.BlockSpec(memory_space=pltpu.SMEM)],
        out_specs=(vmem, vmem, vmem),
        scratch_shapes=[
            pltpu.VMEM((n_fn, cap, slab), BF16),
            pltpu.VMEM((n_fn, cap, slab), BF16),
            pltpu.VMEM((WIDE, slab), BF16),
            pltpu.VMEM((WIDE, slab), BF16),
            pltpu.VMEM((SLOTS, LANES), F32),
            pltpu.VMEM((n_blk * each, LANES), F32),
            pltpu.VMEM((n_blk * each, LANES), F32),
            pltpu.VMEM((2, hy, NX * size_a, LANES), F32),
            pltpu.VMEM((NX - 1, size_a, LANES), F32),
            pltpu.VMEM((2, hx, ny * size_b, LANES), F32),
            pltpu.VMEM((ny - 1, size_b, LANES), F32),
            pltpu.VMEM((WIDE, WIDE), F32),
            pltpu.VMEM((WIDE, WIDE), F32),
            pltpu.VMEM((WIDE, WIDE), F32),
            pltpu.VMEM((WIDE, WIDE), BF16),
            pltpu.VMEM((WIDE, WIDE), BF16),
            pltpu.VMEM((WIDE, WIDE), BF16),
            pltpu.VMEM((WIDE, WIDE), BF16),
            pltpu.VMEM((-(-count // 16) * 16, WIDE), F32),
            pltpu.SemaphoreType.DMA((n_fn - 1,)),
            pltpu.SemaphoreType.DMA((n_fn - 1,)),
            sems(2, hy),
            sems(NX - 1),
            sems(2, hx),
            sems(ny - 1),
            sems(2, hy),
            sems(NX - 1),
            sems(2, hx),
            sems(ny - 1),
        ],
        compiler_params=pltpu.CompilerParams(
            collective_id=0, has_side_effects=True, vmem_limit_bytes=48 * 1024 * 1024
        ),
    )(zone_of.reshape(1, funcs), orbitals, potential, chem_shift)


def solution(mesh):
    placed = (P("fn", "blk"), P("fn", "blk"), P("fn", None), P())
    return jax.shard_map(
        on_device,
        mesh=mesh,
        in_specs=placed,
        out_specs=(P("fn", "blk", None), P("fn", "blk", None), P("fn", "blk", None)),
        check_vma=False,
    )
```

time: 600 us -> 114 us (0.19)
  the two profiles are of different devices: /device:TPU:1 before, /device:TPU:64 now
where the time goes in v1:
time: 114 us
  Pallas kernels  108 us (95%)
  local copies, waits for them, and re-layouts  4.4 us (4%)
  between operations  1.3 us (1%)
    pallas_call x1, Pallas kernels, on_device(): pl.pallas_call(body, out_shape=(out, out, out), in_specs=[vmem, vmem, vme...  108 us
    unnamed x6, local copies, waits for them, and re-layouts  2.4 us

profile of v1, /device:TPU:64, one launch (start us, length us, event | category | flops | bytes accessed | tf_op | source)
XLA Modules:
  0.0 113.9 jit_solution(15936347821780854429)
XLA Ops:
  1.3 0.0 copy-start.2
  1.3 0.7 copy-done.2
  2.0 0.0 copy-start
  2.0 1.0 copy-done
  3.0 0.0 copy-start.1
  3.0 0.7 copy-done.1
  3.7 108.2 %shard_map.67 = (f32[1,18,576]{2,1,0:T(8,128)S(1)}, f32[1,18,576]{2,1,0:T(8,128)S(1)}, f32[1,18,576]{2,1,0:T(8,128)S(1)}) custom-call(s32[1,256]{1,0:T(1,128)S(1)} %bitcast.1, bf16[256,1024]{1,0:T(8,128)(2,1)S(1)} %copy-done, f32[1,1024]{1,0:T(1,128)S(1)} %copy-done.1, f32[1]{0:T(128)S(6)} %copy.10.refs_3_), custom_call_target="tpu_custom_call" | custom-call | tf_op jit(solution)/shard_map/pallas_call | solution.py:417
  111.9 0.7 copy.7
  112.6 0.7 copy.8
  113.2 0.7 copy.9
Async XLA Ops:
  1.3 0.7 copy-start.2
  2.0 1.0 copy-start
  3.0 0.7 copy-start.1

commit v2 on v1

v2 whole, which is shorter than its diff:
```python
import jax
import jax.numpy as jnp
from jax import lax
from jax.experimental import pallas as pl
from jax.experimental.pallas import tpu as pltpu
from jax.sharding import PartitionSpec as P

SLOTS = 576
WIDE = 640
LANES = 128
NX = 4
CORES = 2
BIG = 2.0**100
BF16 = jnp.bfloat16
F32 = jnp.float32

TILES = [
    [(0, 0, 336), (1, 128, 336), (2, 256, 336)],
    [(0, 336, 432), (1, 336, 432), (2, 336, 432), (3, 384, 432)],
    [(0, 432, 528), (1, 432, 528), (2, 432, 528), (3, 432, 528)],
    [(0, 528, 576), (1, 528, 576), (2, 528, 576), (3, 528, 576), (4, 512, 576)],
]


def wrap(value, n):
    return lax.rem(value + n, n)


def rows(start, count):
    return pl.ds(pl.multiple_of(start, 8), count)


def split(value):
    high = value.astype(BF16)
    return high, (value - high.astype(F32)).astype(BF16)


def times(left, right_high, right_low):
    high, low = split(left)
    count = left.shape[0]
    both = jnp.dot(
        jnp.concatenate([high, low], axis=0), right_high[...], preferred_element_type=F32
    )
    return both[:count] + both[count:] + jnp.dot(high, right_low[...], preferred_element_type=F32)


class Ring:
    def __init__(self, n, me, device, base, size):
        self.n, self.me, self.device, self.base, self.size = n, me, device, base, size

    def at(self, offset):
        return self.base + wrap(self.me + offset, self.n) * self.size


def far_first(n):
    return sorted(range(1, n), key=lambda k: -min(k, n - k))


def direct_sum(ring, data, total, landing, send_sem, recv_sem):
    copies = []

    def start():
        for k in far_first(ring.n):
            copies.append(
                pltpu.make_async_remote_copy(
                    src_ref=data.at[rows(ring.at(k), ring.size)],
                    dst_ref=landing.at[k - 1],
                    send_sem=send_sem.at[k - 1],
                    recv_sem=recv_sem.at[k - 1],
                    device_id=ring.device(wrap(ring.me + k, ring.n)),
                )
            )
            copies[-1].start()

    def finish():
        here = rows(ring.at(0), ring.size)
        value = data[here, :]
        for copy, k in zip(copies, far_first(ring.n)):
            copy.wait_recv()
            value = value + landing[k - 1]
        total[here, :] = value

    return start, finish, copies


def direct_gather(ring, data, send_sem, recv_sem):
    sent = []

    def copy(k, offset):
        here = data.at[rows(ring.at(offset), ring.size)]
        return pltpu.make_async_remote_copy(
            src_ref=here,
            dst_ref=here,
            send_sem=send_sem.at[k - 1],
            recv_sem=recv_sem.at[k - 1],
            device_id=ring.device(wrap(ring.me + k, ring.n)),
        )

    def start():
        for k in far_first(ring.n):
            sent.append(copy(k, 0))
            sent[-1].start()

    def finish():
        for k in far_first(ring.n):
            copy(k, -k).wait_recv()

    return start, finish, sent


class Batch:
    def __init__(self, n_x, n_y, x, y, along_x, along_y, size, refs):
        part, gath, land_x, land_y, sum_x, sum_y, get_y, get_x = refs
        self.part, self.gath = part, gath
        ring_x = Ring(n_x, x, along_x, 0, n_y * size)
        ring_y = Ring(n_y, y, along_y, x * (n_y * size), size)
        stages = [
            direct_sum(ring_x, part, part, land_x, sum_x.at[0], sum_x.at[1]),
            direct_sum(ring_y, part, gath, land_y, sum_y.at[0], sum_y.at[1]),
            direct_gather(ring_y, gath, get_y.at[0], get_y.at[1]),
            direct_gather(ring_x, gath, get_x.at[0], get_x.at[1]),
        ]
        self.starts = [s[0] for s in stages]
        self.finishes = [s[1] for s in stages]
        self.sent = [s[2] for s in stages]
        self.stage = 0

    def begin(self):
        self.starts[0]()

    def advance(self):
        self.finishes[self.stage]()
        self.stage += 1
        if self.stage < len(self.starts):
            self.starts[self.stage]()

    def drain(self):
        for copies in self.sent:
            for copy in copies:
                copy.wait_send()


def kernel(
    n_fn, ny, sizes,
    zone_hbm, orb_hbm, pot_hbm, mu_ref, packed,
    zone_ref, orb_ref, pot_ref, in_sem, send, recv, coeffs, weighted, present, place,
    s_full, h_full, l_full, s_high, s_low, l_high, l_low, l_rows,
    z_send, z_recv, *batch_refs,
):
    cap = SLOTS // n_fn
    nz = n_fn // CORES
    deep = CORES * cap
    me = lax.axis_index("fn")
    blk = lax.axis_index("blk")
    my_z, core = me // CORES, lax.rem(me, CORES)
    y, x = blk // NX, lax.rem(blk, NX)

    def along_y(pos):
        return {"blk": pos * NX + x}

    def along_x(pos):
        return {"blk": y * NX + pos}

    def fn_index(dz, dc):
        return wrap(my_z + dz, nz) * CORES + lax.rem(core + dc, CORES)

    barrier = pltpu.get_barrier_semaphore()

    @pl.loop(1, n_fn)
    def _(k):
        pl.semaphore_signal(barrier, inc=1, device_id={"fn": wrap(me + k - n_fn, n_fn)})

    for k in range(1, ny):
        pl.semaphore_signal(barrier, inc=1, device_id=along_y(wrap(y + k, ny)))
    for k in range(1, NX):
        pl.semaphore_signal(barrier, inc=1, device_id=along_x(wrap(x + k, NX)))

    loads = [
        pltpu.make_async_copy(src, dst, in_sem.at[i])
        for i, (src, dst) in enumerate(
            ((zone_hbm, zone_ref), (orb_hbm, orb_ref), (pot_hbm, pot_ref))
        )
    ]
    for load in loads:
        load.start()
    coeffs[...] = jnp.zeros(coeffs.shape, BF16)
    weighted[...] = jnp.zeros(weighted.shape, BF16)

    loads[0].wait()
    funcs = orb_ref.shape[0]
    slab = orb_ref.shape[1]
    zones = zone_ref[...]
    onehot = (zones == lax.broadcasted_iota(jnp.int32, (n_fn, funcs), 0)).astype(F32)
    earlier = (
        lax.broadcasted_iota(jnp.int32, (funcs, funcs), 0)
        < lax.broadcasted_iota(jnp.int32, (funcs, funcs), 1)
    ).astype(F32)
    before = jnp.dot(onehot.astype(BF16), earlier.astype(BF16), preferred_element_type=F32)
    rank = jnp.sum(before * onehot, axis=0, keepdims=True).astype(jnp.int32)
    target = zones * cap + rank
    selector = (target == lax.broadcasted_iota(jnp.int32, (SLOTS, funcs), 0)).astype(F32)
    filled = jnp.sum(selector, axis=1, keepdims=True) > 0.5
    selector = selector.astype(BF16)
    wide = min(256, slab)
    loads[1].wait()
    for c0 in range(0, slab, wide):
        slotted = jnp.dot(selector, orb_ref[:, c0 : c0 + wide], preferred_element_type=F32)
        if c0 == 0:
            slotted = jnp.where(filled, slotted, BIG)
        for zone in range(n_fn):
            send[zone, :, c0 : c0 + wide] = slotted[zone * cap : (zone + 1) * cap].astype(BF16)
    loads[2].wait()

    pl.semaphore_wait(barrier, n_fn - 1 + ny - 1 + NX - 1)

    def near(k):
        return (k + 1) // 2 * (1 if k % 2 else -1)

    z_waiting = []

    def z_copy(k, dc, arriving):
        q = CORES * k + dc - 1
        to = fn_index(near(k), dc)
        return pltpu.make_async_remote_copy(
            src_ref=send.at[to],
            dst_ref=recv.at[fn_index(-near(k), dc) if arriving else me],
            send_sem=z_send.at[q],
            recv_sem=z_recv.at[q],
            device_id={"fn": to},
        )

    def z_start(*chips):
        for k in chips:
            for dc in range(0 if k else 1, CORES):
                z_copy(k, dc, False).start()
                z_waiting.append((k, dc))

    def z_left(*chips):
        for k, dc in [item for item in z_waiting if item[0] in chips]:
            z_copy(k, dc, False).wait_send()
            z_waiting.remove((k, dc))

    def unpack(*chips):
        for k in chips:
            for dc in range(0 if k else 1, CORES):
                z_copy(k, dc, True).wait_recv()
            chip = wrap(my_z - near(k), nz)
            value = jnp.concatenate(
                [recv[chip * CORES + c].astype(F32) for c in range(CORES)], axis=0
            )
            marks = value[:, :1] < 0.5 * BIG
            value = jnp.where(marks, value, 0.0)
            here = slice(k * deep, (k + 1) * deep)
            coeffs[here, :] = value.astype(BF16)
            weighted[here, :] = (pot_ref[...] * value).astype(BF16)
            present[here, :] = jnp.broadcast_to(marks.astype(F32), (deep, LANES))

    batches = [
        Batch(NX, ny, x, y, along_x, along_y, size, batch_refs[8 * i : 8 * i + 8])
        for i, size in enumerate(sizes)
    ]

    def share(i):
        part = batches[i].part
        tiles = TILES[i]
        low = min(r0 for _, r0, _ in tiles)
        high = max(r1 for _, _, r1 in tiles)
        span = LANES * (tiles[-1][0] + 1)
        mine, mine_w = coeffs[low:high, :], weighted[low:high, :]
        count = high - low
        over = (((1,), (1,)), ((), ()))
        at = 0
        for c0 in range(0, span, 256):
            c1 = min(c0 + 256, span)
            both = lax.dot_general(
                jnp.concatenate([mine, mine_w], axis=0), coeffs[c0:c1, :], over,
                preferred_element_type=F32,
            )
            other = lax.dot_general(mine, weighted[c0:c1, :], over, preferred_element_type=F32)
            gram, ham = both[:count], 0.5 * (both[count:] + other)
            for j, r0, r1 in tiles:
                if c0 <= LANES * j < c1:
                    cols = slice(LANES * j - c0, LANES * (j + 1) - c0)
                    part[at : at + r1 - r0, :] = gram[r0 - low : r1 - low, cols]
                    at += r1 - r0
                    part[at : at + r1 - r0, :] = ham[r0 - low : r1 - low, cols]
                    at += r1 - r0
        if at < part.shape[0]:
            part[at:, :] = jnp.zeros((part.shape[0] - at, LANES), F32)
        batches[i].begin()

    def collect(i):
        at = 0
        for j, r0, r1 in TILES[i]:
            cols = slice(LANES * j, LANES * (j + 1))
            s_full[r0:r1, cols] = batches[i].gath[at : at + r1 - r0, :]
            at += r1 - r0
            h_full[r0:r1, cols] = batches[i].gath[at : at + r1 - r0, :]
            at += r1 - r0

    def advance(*order):
        for i in order:
            batches[i].advance()
            if batches[i].stage == 4:
                collect(i)

    def place_columns():
        p = lax.broadcasted_iota(jnp.int32, (WIDE, 1), 0)
        k = p // deep
        dz = (k + 1) // 2 * (2 * lax.rem(k, 2) - 1)
        slot = lax.rem(my_z - dz + nz, nz) * deep + p - k * deep
        slot = jnp.where(p < SLOTS, slot, p)
        place[...] = (slot == lax.broadcasted_iota(jnp.int32, (WIDE, WIDE), 1)).astype(F32).astype(BF16)

    z_start(0, 1, 2, 3, 4)
    recv[me] = send[me]
    place_columns()
    present[SLOTS:, :] = jnp.zeros((WIDE - SLOTS, LANES), F32)
    s_full[SLOTS:, :] = jnp.zeros((WIDE - SLOTS, WIDE), F32)
    h_full[SLOTS:, :] = jnp.zeros((WIDE - SLOTS, WIDE), F32)
    l_rows[...] = jnp.zeros(l_rows.shape, F32)
    unpack(0)
    z_left(1, 2)
    z_start(5, 6)
    unpack(1, 2)
    z_left(3, 4)
    z_start(7, 8)
    unpack(3, 4)
    z_left(5, 6)
    z_start(9, 10)
    unpack(5, 6)
    share(0)
    z_left(7, 8)
    z_start(11)
    advance(0)
    unpack(7, 8)
    share(1)
    advance(0, 1)
    unpack(9, 10)
    share(2)
    advance(0, 1, 2, 1)
    unpack(11)
    share(3)
    advance(0, 2, 3, 1, 2, 3, 2, 3, 3)

    mu = mu_ref[0]
    down = lax.broadcasted_iota(jnp.int32, (LANES, LANES), 0)
    across = lax.broadcasted_iota(jnp.int32, (LANES, LANES), 1)
    for i in range(5):
        here = slice(LANES * i, LANES * (i + 1))
        for j in range(i + 1):
            there = slice(LANES * j, LANES * (j + 1))
            s_block, h_block = s_full[here, there], h_full[here, there]
            if i == j:
                s_block = jnp.where(down >= across, s_block, s_block.T)
                h_block = jnp.where(down >= across, h_block, h_block.T)
            l_block = -0.5 * (h_block - mu * s_block)
            if i == j:
                l_block = l_block + jnp.where(down == across, 0.5 * present[here, :], 0.0)
                s_full[here, there] = s_block
                h_full[here, there] = h_block
            l_full[here, there] = l_block
            if i > j:
                s_full[there, here] = s_block.T
                h_full[there, here] = h_block.T
                l_full[there, here] = l_block.T

    count = packed.shape[1]
    room = l_rows.shape[1]
    for i in range(count):
        slot = blk * count + i
        chip = slot // deep
        dz = wrap(my_z - chip, nz)
        far = (dz + nz // 2 - 1) // nz
        k = (1 - far) * (2 * dz - (dz + nz - 1) // nz) + far * (2 * nz - 2 * dz)
        row = pl.ds(k * deep + slot - chip * deep, 1)
        l_rows[0, i : i + 1, :] = l_full[row, :]
        l_rows[1, i : i + 1, :] = s_full[row, :]
        l_rows[2, i : i + 1, :] = h_full[row, :]
    for i in range(5):
        here = slice(LANES * i, LANES * (i + 1))
        s_high[here, :], s_low[here, :] = split(s_full[here, :])
        l_high[here, :], l_low[here, :] = split(l_full[here, :])

    product = times(l_rows[0], s_high, s_low)
    square = times(product, l_high, l_low)
    cubed = times(times(square, s_high, s_low), l_high, l_low)

    result = jnp.concatenate([l_rows[1], l_rows[2], 3.0 * square - 2.0 * cubed], axis=0)
    high, rest = result.astype(BF16), result - result.astype(BF16).astype(F32)
    middle, low = split(rest)
    placed = jnp.dot(
        jnp.concatenate([high, middle, low], axis=0), place[...], preferred_element_type=F32
    )
    placed = placed[: 3 * room] + placed[3 * room : 6 * room] + placed[6 * room :]
    for i in range(3):
        packed[i] = placed[i * room : i * room + count, :SLOTS].reshape(count, 1, SLOTS)

    z_left(*range(nz))
    for batch in batches:
        batch.drain()


def hand_out(packed, *outs):
    for i, out in enumerate(outs):
        out[...] = packed[i]


def on_device(orbitals, potential, zone_of, chem_shift):
    n_fn = lax.axis_size("fn")
    n_blk = lax.axis_size("blk")
    ny = n_blk // NX
    cap = SLOTS // n_fn
    funcs, slab = orbitals.shape
    count = SLOTS // n_blk
    sizes = [
        -(-2 * sum(r1 - r0 for _, r0, r1 in tiles) // (n_blk * 8)) * 8 for tiles in TILES
    ]
    batch_scratch = []
    for size in sizes:
        batch_scratch += [
            pltpu.VMEM((n_blk * size, LANES), F32),
            pltpu.VMEM((n_blk * size, LANES), F32),
            pltpu.VMEM((max(1, NX - 1), ny * size, LANES), F32),
            pltpu.VMEM((ny - 1, size, LANES), F32),
        ] + [pltpu.SemaphoreType.DMA((2, max(1, n - 1))) for n in (NX, ny, ny, NX)]

    out = jax.ShapeDtypeStruct((count, 1, SLOTS), F32)
    vmem = pl.BlockSpec(memory_space=pltpu.VMEM)
    hbm = pl.BlockSpec(memory_space=pltpu.HBM)

    def body(*refs):
        kernel(n_fn, ny, sizes, *refs)

    packed = pl.pallas_call(
        body,
        out_shape=jax.ShapeDtypeStruct((3, count, 1, SLOTS), F32),
        in_specs=[hbm, hbm, hbm, pl.BlockSpec(memory_space=pltpu.SMEM)],
        out_specs=vmem,
        scratch_shapes=[
            pltpu.VMEM((1, funcs), jnp.int32),
            pltpu.VMEM((funcs, slab), BF16),
            pltpu.VMEM((1, slab), F32),
            pltpu.SemaphoreType.DMA((3,)),
            pltpu.VMEM((n_fn, cap, slab), BF16),
            pltpu.VMEM((n_fn, cap, slab), BF16),
            pltpu.VMEM((WIDE, slab), BF16),
            pltpu.VMEM((WIDE, slab), BF16),
            pltpu.VMEM((WIDE, LANES), F32),
            pltpu.VMEM((WIDE, WIDE), BF16),
            pltpu.VMEM((WIDE, WIDE), F32),
            pltpu.VMEM((WIDE, WIDE), F32),
            pltpu.VMEM((WIDE, WIDE), F32),
            pltpu.VMEM((WIDE, WIDE), BF16),
            pltpu.VMEM((WIDE, WIDE), BF16),
            pltpu.VMEM((WIDE, WIDE), BF16),
            pltpu.VMEM((WIDE, WIDE), BF16),
            pltpu.VMEM((3, -(-count // 16) * 16, WIDE), F32),
            pltpu.SemaphoreType.DMA((n_fn - 1,)),
            pltpu.SemaphoreType.DMA((n_fn - 1,)),
            *batch_scratch,
        ],
        compiler_params=pltpu.CompilerParams(
            collective_id=0, has_side_effects=True, vmem_limit_bytes=60 * 1024 * 1024
        ),
    )(zone_of.reshape(1, funcs), orbitals, potential, chem_shift)
    results = pl.pallas_call(
        hand_out,
        out_shape=(out, out, out),
        in_specs=[vmem],
        out_specs=(vmem, vmem, vmem),
    )(packed)
    return tuple(jnp.transpose(result, (1, 0, 2)) for result in results)


def solution(mesh):
    placed = (P("fn", "blk"), P("fn", "blk"), P("fn", None), P())
    return jax.shard_map(
        on_device,
        mesh=mesh,
        in_specs=placed,
        out_specs=(P("fn", "blk", None), P("fn", "blk", None), P("fn", "blk", None)),
        check_vma=False,
    )
```

time: 114 us -> 98.6 us (0.86)
  the two profiles are of different devices: /device:TPU:64 before, /device:TPU:1 now
where the time goes in v2:
time: 98.6 us; the launch traced here: 97.7 us
  Pallas kernels  96.4 us (98%)
  between operations  1.29 us (1%)
    pallas_call x1, Pallas kernels, on_device(): pl.pallas_call(body, out_shape=jax.ShapeDtypeStruct((3, count, 1, SLOTS),...  94.8 us

profile of v2, /device:TPU:1, one launch (start us, length us, event | category | flops | bytes accessed | tf_op | source)
XLA Modules:
  0.0 97.7 jit_solution(14900297322183702742)
XLA Ops:
  1.3 94.8 %shard_map.67.packed = f32[3,18,1,576]{3,2,1,0:T(1,128)} custom-call(s32[1,256]{1,0:T(1,128)} %bitcast.4, bf16[256,1024]{1,0:T(8,128)(2,1)} %refs_1_.1, f32[1,1024]{1,0:T(1,128)} %refs_2_.1, f32[1]{0:T(128)S(6)} %copy.7.refs_3_), custom_call_target="tpu_custom_call" | custom-call | tf_op jit(solution)/shard_map/pallas_call | solution.py:435
  96.1 1.6 %shard_map.68 = (f32[18,1,576]{2,1,0:T(1,128)}, f32[18,1,576]{2,1,0:T(1,128)}, f32[18,1,576]{2,1,0:T(1,128)}) custom-call(f32[3,18,1,576]{3,2,1,0:T(1,128)} %shard_map.67.packed), custom_call_target="tpu_custom_call" | custom-call | tf_op jit(solution)/shard_map/pallas_call | solution.py:467

commit v3 on v2

--- a/solution.py
+++ b/solution.py
@@ -15,8 +15,9 @@
 F32 = jnp.float32
 
 TILES = [
-    [(0, 0, 336), (1, 128, 336), (2, 256, 336)],
-    [(0, 336, 432), (1, 336, 432), (2, 336, 432), (3, 384, 432)],
+    [(0, 0, 240), (1, 128, 240)],
+    [(0, 240, 336), (1, 240, 336), (2, 272, 336)],
+    [(0, 336, 432), (1, 336, 432), (2, 256, 272), (2, 336, 432), (3, 384, 432)],
     [(0, 432, 528), (1, 432, 528), (2, 432, 528), (3, 432, 528)],
     [(0, 528, 576), (1, 528, 576), (2, 528, 576), (3, 528, 576), (4, 512, 576)],
 ]
@@ -183,9 +184,6 @@
     ]
     for load in loads:
         load.start()
-    coeffs[...] = jnp.zeros(coeffs.shape, BF16)
-    weighted[...] = jnp.zeros(weighted.shape, BF16)
-
     loads[0].wait()
     funcs = orb_ref.shape[0]
     slab = orb_ref.shape[1]
@@ -198,20 +196,8 @@
     before = jnp.dot(onehot.astype(BF16), earlier.astype(BF16), preferred_element_type=F32)
     rank = jnp.sum(before * onehot, axis=0, keepdims=True).astype(jnp.int32)
     target = zones * cap + rank
-    selector = (target == lax.broadcasted_iota(jnp.int32, (SLOTS, funcs), 0)).astype(F32)
-    filled = jnp.sum(selector, axis=1, keepdims=True) > 0.5
-    selector = selector.astype(BF16)
-    wide = min(256, slab)
     loads[1].wait()
-    for c0 in range(0, slab, wide):
-        slotted = jnp.dot(selector, orb_ref[:, c0 : c0 + wide], preferred_element_type=F32)
-        if c0 == 0:
-            slotted = jnp.where(filled, slotted, BIG)
-        for zone in range(n_fn):
-            send[zone, :, c0 : c0 + wide] = slotted[zone * cap : (zone + 1) * cap].astype(BF16)
     loads[2].wait()
-
-    pl.semaphore_wait(barrier, n_fn - 1 + ny - 1 + NX - 1)
 
     def near(k):
         return (k + 1) // 2 * (1 if k % 2 else -1)
@@ -229,16 +215,28 @@
             device_id={"fn": to},
         )
 
-    def z_start(*chips):
+    def z_start(chips, cores):
         for k in chips:
-            for dc in range(0 if k else 1, CORES):
+            for dc in cores:
                 z_copy(k, dc, False).start()
                 z_waiting.append((k, dc))
 
-    def z_left(*chips):
-        for k, dc in [item for item in z_waiting if item[0] in chips]:
-            z_copy(k, dc, False).wait_send()
-            z_waiting.remove((k, dc))
+    def z_left(chips, cores):
+        for k in chips:
+            for dc in cores:
+                z_copy(k, dc, False).wait_send()
+                z_waiting.remove((k, dc))
+
+    def fill(*chips):
+        for k in chips:
+            chip = wrap(my_z + near(k), nz)
+            slot = lax.broadcasted_iota(jnp.int32, (deep, funcs), 0) + chip * deep
+            selector = (target == slot).astype(F32)
+            filled = jnp.sum(selector, axis=1, keepdims=True) > 0.5
+            block = jnp.dot(selector.astype(BF16), orb_ref[...], preferred_element_type=F32)
+            block = jnp.where(filled, block, BIG)
+            for c in range(CORES):
+                send[chip * CORES + c] = block[c * cap : (c + 1) * cap].astype(BF16)
 
     def unpack(*chips):
         for k in chips:
@@ -312,41 +310,11 @@
         slot = jnp.where(p < SLOTS, slot, p)
         place[...] = (slot == lax.broadcasted_iota(jnp.int32, (WIDE, WIDE), 1)).astype(F32).astype(BF16)
 
-    z_start(0, 1, 2, 3, 4)
-    recv[me] = send[me]
-    place_columns()
-    present[SLOTS:, :] = jnp.zeros((WIDE - SLOTS, LANES), F32)
-    s_full[SLOTS:, :] = jnp.zeros((WIDE - SLOTS, WIDE), F32)
-    h_full[SLOTS:, :] = jnp.zeros((WIDE - SLOTS, WIDE), F32)
-    l_rows[...] = jnp.zeros(l_rows.shape, F32)
-    unpack(0)
-    z_left(1, 2)
-    z_start(5, 6)
-    unpack(1, 2)
-    z_left(3, 4)
-    z_start(7, 8)
-    unpack(3, 4)
-    z_left(5, 6)
-    z_start(9, 10)
-    unpack(5, 6)
-    share(0)
-    z_left(7, 8)
-    z_start(11)
-    advance(0)
-    unpack(7, 8)
-    share(1)
-    advance(0, 1)
-    unpack(9, 10)
-    share(2)
-    advance(0, 1, 2, 1)
-    unpack(11)
-    share(3)
-    advance(0, 2, 3, 1, 2, 3, 2, 3, 3)
-
     mu = mu_ref[0]
     down = lax.broadcasted_iota(jnp.int32, (LANES, LANES), 0)
     across = lax.broadcasted_iota(jnp.int32, (LANES, LANES), 1)
-    for i in range(5):
+
+    def assemble(i):
         here = slice(LANES * i, LANES * (i + 1))
         for j in range(i + 1):
             there = slice(LANES * j, LANES * (j + 1))
@@ -359,11 +327,71 @@
                 l_block = l_block + jnp.where(down == across, 0.5 * present[here, :], 0.0)
                 s_full[here, there] = s_block
                 h_full[here, there] = h_block
-            l_full[here, there] = l_block
-            if i > j:
+            else:
                 s_full[there, here] = s_block.T
                 h_full[there, here] = h_block.T
-                l_full[there, here] = l_block.T
+                l_block_t = l_block.T
+                l_full[there, here] = l_block_t
+                s_high[there, here], s_low[there, here] = split(s_block.T)
+                l_high[there, here], l_low[there, here] = split(l_block_t)
+            l_full[here, there] = l_block
+            s_high[here, there], s_low[here, there] = split(s_block)
+            l_high[here, there], l_low[here, there] = split(l_block)
+
+    fill(1, 2)
+    pl.semaphore_wait(barrier, n_fn - 1 + ny - 1 + NX - 1)
+    every = range(CORES)
+    z_start((1, 2), every)
+    fill(3, 4)
+    z_start((3, 4), every)
+    fill(0)
+    z_start((0,), every[1:])
+    recv[me] = send[me]
+    fill(*range(5, nz))
+    coeffs[...] = jnp.zeros(coeffs.shape, BF16)
+    weighted[...] = jnp.zeros(weighted.shape, BF16)
+    place_columns()
+    present[SLOTS:, :] = jnp.zeros((WIDE - SLOTS, LANES), F32)
+    s_full[SLOTS:, :] = jnp.zeros((WIDE - SLOTS, WIDE), F32)
+    h_full[SLOTS:, :] = jnp.zeros((WIDE - SLOTS, WIDE), F32)
+    l_rows[...] = jnp.zeros(l_rows.shape, F32)
+    half, other = every[:1], every[1:]
+    z_left((1, 2), every)
+    z_start((5, 6), half)
+    z_left((3, 4), every)
+    z_start((5, 6), other)
+    unpack(0, 1, 2, 3, 4)
+    share(0)
+    z_left((5, 6), half)
+    z_start((7, 8), half)
+    z_left((5, 6), other)
+    z_start((7, 8), other)
+    unpack(5, 6)
+    share(1)
+    z_left((7, 8), half)
+    z_start((9, 10), half)
+    advance(0)
+    z_left((7, 8), other)
+    z_start((9, 10), other)
+    unpack(7, 8)
+    advance(1)
+    share(2)
+    advance(0)
+    z_left((9, 10), half)
+    z_start((11,), half)
+    advance(1, 0)
+    z_left((9, 10), other)
+    z_start((11,), other)
+    unpack(9, 10)
+    share(3)
+    advance(2, 1, 0, 2)
+    unpack(11)
+    share(4)
+    advance(1, 3, 2, 4, 3, 4, 2, 3, 4, 3)
+    for i in range(4):
+        assemble(i)
+    advance(4)
+    assemble(4)
 
     count = packed.shape[1]
     room = l_rows.shape[1]
@@ -377,11 +405,6 @@
         l_rows[0, i : i + 1, :] = l_full[row, :]
         l_rows[1, i : i + 1, :] = s_full[row, :]
         l_rows[2, i : i + 1, :] = h_full[row, :]
-    for i in range(5):
-        here = slice(LANES * i, LANES * (i + 1))
-        s_high[here, :], s_low[here, :] = split(s_full[here, :])
-        l_high[here, :], l_low[here, :] = split(l_full[here, :])
-
     product = times(l_rows[0], s_high, s_low)
     square = times(product, l_high, l_low)
     cubed = times(times(square, s_high, s_low), l_high, l_low)
@@ -396,7 +419,8 @@
     for i in range(3):
         packed[i] = placed[i * room : i * room + count, :SLOTS].reshape(count, 1, SLOTS)
 
-    z_left(*range(nz))
+    for k, dc in list(z_waiting):
+        z_left((k,), (dc,))
     for batch in batches:
         batch.drain()
 

time: 98.6 us -> 95.2 us (0.966)
  Pallas kernels: 96.4 us -> 93.7 us
    pallas_call x1, Pallas kernels: 94.8 us -> 92.2 us  [on_device(): pl.pallas_call(body, out_shape=jax.ShapeDtypeStruct((3, count, 1, SLOTS),...]
where the time goes in v3:
time: 95.2 us; the launch traced here: 95 us
  Pallas kernels  93.7 us (98%)
  between operations  1.29 us (1%)
    pallas_call x1, Pallas kernels, on_device(): pl.pallas_call(body, out_shape=jax.ShapeDtypeStruct((3, count, 1, SLOTS),...  92.2 us

profile of v3, /device:TPU:1, one launch (start us, length us, event | category | flops | bytes accessed | tf_op | source)
XLA Modules:
  0.0 95.0 jit_solution(10282448575480930957)
XLA Ops:
  1.3 92.2 %shard_map.67.packed = f32[3,18,1,576]{3,2,1,0:T(1,128)} custom-call(s32[1,256]{1,0:T(1,128)} %bitcast.4, bf16[256,1024]{1,0:T(8,128)(2,1)} %refs_1_.1, f32[1,1024]{1,0:T(1,128)} %refs_2_.1, f32[1]{0:T(128)S(6)} %copy.7.refs_3_), custom_call_target="tpu_custom_call" | custom-call | tf_op jit(solution)/shard_map/pallas_call | solution.py:459
  93.4 1.6 %shard_map.68 = (f32[18,1,576]{2,1,0:T(1,128)}, f32[18,1,576]{2,1,0:T(1,128)}, f32[18,1,576]{2,1,0:T(1,128)}) custom-call(f32[3,18,1,576]{3,2,1,0:T(1,128)} %shard_map.67.packed), custom_call_target="tpu_custom_call" | custom-call | tf_op jit(solution)/shard_map/pallas_call | solution.py:491

commit v4 on v3

--- a/solution.py
+++ b/solution.py
@@ -135,9 +135,9 @@
         if self.stage < len(self.starts):
             self.starts[self.stage]()
 
-    def drain(self):
-        for copies in self.sent:
-            for copy in copies:
+    def drain(self, stages):
+        for stage in stages:
+            for copy in self.sent[stage]:
                 copy.wait_send()
 
 
@@ -165,17 +165,6 @@
     def fn_index(dz, dc):
         return wrap(my_z + dz, nz) * CORES + lax.rem(core + dc, CORES)
 
-    barrier = pltpu.get_barrier_semaphore()
-
-    @pl.loop(1, n_fn)
-    def _(k):
-        pl.semaphore_signal(barrier, inc=1, device_id={"fn": wrap(me + k - n_fn, n_fn)})
-
-    for k in range(1, ny):
-        pl.semaphore_signal(barrier, inc=1, device_id=along_y(wrap(y + k, ny)))
-    for k in range(1, NX):
-        pl.semaphore_signal(barrier, inc=1, device_id=along_x(wrap(x + k, NX)))
-
     loads = [
         pltpu.make_async_copy(src, dst, in_sem.at[i])
         for i, (src, dst) in enumerate(
@@ -184,6 +173,18 @@
     ]
     for load in loads:
         load.start()
+
+    barrier = pltpu.get_barrier_semaphore()
+
+    @pl.loop(1, n_fn)
+    def _(k):
+        pl.semaphore_signal(barrier, inc=1, device_id={"fn": wrap(me + k - n_fn, n_fn)})
+
+    for k in range(1, ny):
+        pl.semaphore_signal(barrier, inc=1, device_id=along_y(wrap(y + k, ny)))
+    for k in range(1, NX):
+        pl.semaphore_signal(barrier, inc=1, device_id=along_x(wrap(x + k, NX)))
+
     loads[0].wait()
     funcs = orb_ref.shape[0]
     slab = orb_ref.shape[1]
@@ -384,12 +385,17 @@
     z_start((11,), other)
     unpack(9, 10)
     share(3)
-    advance(2, 1, 0, 2)
+    advance(2, 0)
     unpack(11)
     share(4)
-    advance(1, 3, 2, 4, 3, 4, 2, 3, 4, 3)
+    advance(1, 2, 3, 4, 1, 2, 3, 4, 3, 2, 4, 3)
     for i in range(4):
         assemble(i)
+    for k, dc in list(z_waiting):
+        z_left((k,), (dc,))
+    for batch in batches[:4]:
+        batch.drain(range(4))
+    batches[4].drain(range(3))
     advance(4)
     assemble(4)
 
@@ -419,10 +425,7 @@
     for i in range(3):
         packed[i] = placed[i * room : i * room + count, :SLOTS].reshape(count, 1, SLOTS)
 
-    for k, dc in list(z_waiting):
-        z_left((k,), (dc,))
-    for batch in batches:
-        batch.drain()
+    batches[4].drain((3,))
 
 
 def hand_out(packed, *outs):

time: 95.2 us -> 94.5 us (level)
  no operation moved by 1% of the time
where the time goes in v4:
time: 94.5 us; the launch traced here: 94.3 us
  Pallas kernels  93 us (98%)
  between operations  1.29 us (1%)
    pallas_call x1, Pallas kernels, on_device(): pl.pallas_call(body, out_shape=jax.ShapeDtypeStruct((3, count, 1, SLOTS),...  91.5 us

profile of v4, /device:TPU:1, one launch (start us, length us, event | category | flops | bytes accessed | tf_op | source)
XLA Modules:
  0.0 94.3 jit_solution(13531288873340198712)
XLA Ops:
  1.3 91.5 %shard_map.67.packed = f32[3,18,1,576]{3,2,1,0:T(1,128)} custom-call(s32[1,256]{1,0:T(1,128)} %bitcast.4, bf16[256,1024]{1,0:T(8,128)(2,1)} %refs_1_.1, f32[1,1024]{1,0:T(1,128)} %refs_2_.1, f32[1]{0:T(128)S(6)} %copy.7.refs_3_), custom_call_target="tpu_custom_call" | custom-call | tf_op jit(solution)/shard_map/pallas_call | solution.py:462
  92.7 1.6 %shard_map.68 = (f32[18,1,576]{2,1,0:T(1,128)}, f32[18,1,576]{2,1,0:T(1,128)}, f32[18,1,576]{2,1,0:T(1,128)}) custom-call(f32[3,18,1,576]{3,2,1,0:T(1,128)} %shard_map.67.packed), custom_call_target="tpu_custom_call" | custom-call | tf_op jit(solution)/shard_map/pallas_call | solution.py:494

commit v5 on v4

--- a/solution.py
+++ b/solution.py
@@ -348,7 +348,13 @@
     fill(0)
     z_start((0,), every[1:])
     recv[me] = send[me]
-    fill(*range(5, nz))
+    half, other = every[:1], every[1:]
+    fill(5, 6)
+    z_left((1, 2), every)
+    z_start((5, 6), half)
+    fill(*range(7, nz))
+    z_left((3, 4), every)
+    z_start((5, 6), other)
     coeffs[...] = jnp.zeros(coeffs.shape, BF16)
     weighted[...] = jnp.zeros(weighted.shape, BF16)
     place_columns()
@@ -356,11 +362,6 @@
     s_full[SLOTS:, :] = jnp.zeros((WIDE - SLOTS, WIDE), F32)
     h_full[SLOTS:, :] = jnp.zeros((WIDE - SLOTS, WIDE), F32)
     l_rows[...] = jnp.zeros(l_rows.shape, F32)
-    half, other = every[:1], every[1:]
-    z_left((1, 2), every)
-    z_start((5, 6), half)
-    z_left((3, 4), every)
-    z_start((5, 6), other)
     unpack(0, 1, 2, 3, 4)
     share(0)
     z_left((5, 6), half)

time: 94.5 us -> 94.9 us (level)
  no operation moved by 1% of the time
where the time goes in v5:
time: 94.9 us; the launch traced here: 94.8 us
  Pallas kernels  93.5 us (99%)
  between operations  1.29 us (1%)
    pallas_call x1, Pallas kernels, on_device(): pl.pallas_call(body, out_shape=jax.ShapeDtypeStruct((3, count, 1, SLOTS),...  91.9 us

profile of v5, /device:TPU:1, one launch (start us, length us, event | category | flops | bytes accessed | tf_op | source)
XLA Modules:
  0.0 94.8 jit_solution(7895759544140237939)
XLA Ops:
  1.3 91.9 %shard_map.67.packed = f32[3,18,1,576]{3,2,1,0:T(1,128)} custom-call(s32[1,256]{1,0:T(1,128)} %bitcast.4, bf16[256,1024]{1,0:T(8,128)(2,1)} %refs_1_.1, f32[1,1024]{1,0:T(1,128)} %refs_2_.1, f32[1]{0:T(128)S(6)} %copy.7.refs_3_), custom_call_target="tpu_custom_call" | custom-call | tf_op jit(solution)/shard_map/pallas_call | solution.py:463
  93.2 1.6 %shard_map.68 = (f32[18,1,576]{2,1,0:T(1,128)}, f32[18,1,576]{2,1,0:T(1,128)}, f32[18,1,576]{2,1,0:T(1,128)}) custom-call(f32[3,18,1,576]{3,2,1,0:T(1,128)} %shard_map.67.packed), custom_call_target="tpu_custom_call" | custom-call | tf_op jit(solution)/shard_map/pallas_call | solution.py:495
